TPU v7x, 32 devices: a whole 2x2x4 slice. The times are simulated.
32 devices in a mesh: win: 2 (over y), lon: 8 (over z, x), lat: 2 (over core).
Axes of the slice: x: 2, y: 2, z: 4, core: 2. Of those that a mesh axis runs over, the one named last changes fastest.
Arguments:
- dual_state: float32 [2, 16, 2, 4096], P('win', None, 'lat', 'lon'), may hold values from -6 to 6
- dual_obs: float32 [2, 16, 2, 4096], P('win', None, 'lat', 'lon'), may hold values from -6 to 6
- increment: float32 [2, 16, 2, 4096], P('win', None, 'lat', 'lon'), may hold values from -6 to 6
- resid_dual: float32 [2, 16, 2, 4096], P('win', None, 'lat', 'lon'), may hold values from -6 to 6
- resid_obs: float32 [2, 16, 2, 4096], P('win', None, 'lat', 'lon'), may hold values from -6 to 6
- resid_incr: float32 [2, 16, 2, 4096], P('win', None, 'lat', 'lon'), may hold values from -6 to 6
- search_dual: float32 [2, 16, 2, 4096], P('win', None, 'lat', 'lon'), may hold values from -6 to 6
- search_obs: float32 [2, 16, 2, 4096], P('win', None, 'lat', 'lon'), may hold values from -6 to 6
- search_incr: float32 [2, 16, 2, 4096], P('win', None, 'lat', 'lon'), may hold values from -6 to 6
- ensemble: bfloat16 [2, 64, 16, 2, 4096], P('win', None, None, 'lat', 'lon'), may hold values from -12 to 12
- tangent_coefs: float32 [2, 5, 16, 2, 4096], P('win', None, None, 'lat', 'lon'), may hold values from -0.25 to 0.25
- obs_weight: float32 [2, 16, 2, 4096], P('win', None, 'lat', 'lon'), may hold values from 0.25 to 2
- obs_var: float32 [2, 16, 2, 4096], P('win', None, 'lat', 'lon'), may hold values from 0.5 to 2
- loc_cols: int32 [8, 5], P('lon'), may hold values from 0 to 7, as said below
- loc_vals: bfloat16 [8, 5, 512, 512], P('lon'), may hold values from -0.125 to 0.125
Outputs:
- next_dual: float32 [2, 16, 2, 4096], P('win', None, 'lat', 'lon')
- next_obs: float32 [2, 16, 2, 4096], P('win', None, 'lat', 'lon')
- next_incr: float32 [2, 16, 2, 4096], P('win', None, 'lat', 'lon')
- next_res_dual: float32 [2, 16, 2, 4096], P('win', None, 'lat', 'lon')
- next_res_obs: float32 [2, 16, 2, 4096], P('win', None, 'lat', 'lon')
- next_res_incr: float32 [2, 16, 2, 4096], P('win', None, 'lat', 'lon')
Inputs may be any that keep to these rules, and one draw needn't show every extreme that they name: `loc_cols`: row block i names 5 distinct column blocks, block i itself among them, each within 3 blocks of i around the longitude loop.
All inputs are finite; a program needn't handle non-finite values.
Results may differ from a plain program's by a relative error of at most 0.0017.
Values may be sent and summed in bfloat16 or wider, within the bound.
A program may use at most 64 MiB of HBM per device.

v0:
```python
import jax
import jax.numpy as jnp
from jax import lax
from jax.sharding import PartitionSpec as P

REACH = 3


def extended_2(array, sides, width, wrap):
    for axis, dim in sides:
        peers, length = (lax.axis_size(axis), array.shape[dim])
        up = [(i, (i + 1) % peers) for i in range(peers if wrap else peers - 1)]
        down = [(j, i) for i, j in up]
        last = lax.slice_in_dim(array, length - width, length, axis=dim)
        leading = lax.slice_in_dim(array, 0, width, axis=dim)
        before = lax.ppermute(last, axis, up)
        after = lax.ppermute(leading, axis, down)
        array = jnp.concatenate([before, array, after], axis=dim)
    return array


def passed_along(block, axis, distance):
    devices = range(lax.axis_size(axis))
    route = [((i - distance) % len(devices), i) for i in devices]
    return lax.ppermute(block, axis, route)


def shifted(value, axis, steps):
    count = lax.axis_size(axis)
    leading, last = (max(0, -steps), min(count, count - steps))
    return lax.ppermute(value, axis, [(source, source + steps) for source in range(leading, last)])


def lon_rim(field, width):
    return extended_2(field, (("lon", 3),), width, True)


def lat_rim(field):
    return extended_2(field, (("lat", 2),), 1, False)


def forward_step(extended, coeff):
    inner = coeff[:, :, 1:-1, 1:-1]
    return (
        (0.5 + inner[0]) * extended[:, 1:-1, 1:-1]
        + inner[1] * extended[:, 1:-1, 2:]
        + inner[2] * extended[:, 1:-1, :-2]
        + inner[3] * extended[:, 2:, 1:-1]
        + inner[4] * extended[:, :-2, 1:-1]
    )


def adjoint_step(extended, coeff):
    scaled = coeff * extended[None]
    return (
        (0.5 + coeff[0, :, 1:-1, 1:-1]) * extended[:, 1:-1, 1:-1]
        + scaled[1, :, 1:-1, :-2]
        + scaled[2, :, 1:-1, 2:]
        + scaled[3, :, :-2, 1:-1]
        + scaled[4, :, 2:, 1:-1]
    )


def propagate(field, coeff_wide, stepper):
    coeff_one = coeff_wide[..., 1:-1]
    first = stepper(lat_rim(lon_rim(field, 1))[0], coeff_one)
    return stepper(lat_rim(lon_rim(first[None], 1))[0], coeff_one)


def localize(members, search, loc_cols, loc_vals):
    count_members = members.shape[0]
    block = members.shape[-1]
    products = (members * search[None]).astype(jnp.bfloat16)
    flat = products.reshape(-1, block)
    bands = lax.axis_size("lon")
    here = lax.axis_index("lon")
    columns = loc_cols[0]
    tiles = loc_vals[0]

    def weight_for(offset):
        target = (here + offset + bands) % bands
        match = (columns == target).astype(jnp.bfloat16)
        return jnp.einsum("j,jpq->pq", match, tiles, preferred_element_type=jnp.float32).astype(
            jnp.bfloat16
        )

    total = jnp.dot(flat, weight_for(0), preferred_element_type=jnp.float32)
    east_side = flat
    west_side = flat
    for distance in range(1, REACH + 1):
        east_side = passed_along(east_side, "lon", -1)
        total = total + jnp.dot(east_side, weight_for(distance), preferred_element_type=jnp.float32)
        west_side = passed_along(west_side, "lon", 1)
        total = total + jnp.dot(
            west_side, weight_for(-distance), preferred_element_type=jnp.float32
        )
    spread = total.reshape(products.shape)
    return jnp.sum(members * spread, axis=0) / (count_members - 1)


def local(
    dual_state,
    dual_obs,
    increment,
    resid_dual,
    resid_obs,
    resid_incr,
    search_dual,
    search_obs,
    search_incr,
    ensemble,
    tangent_coefs,
    obs_weight,
    obs_var,
    loc_cols,
    loc_vals,
):
    coeff_wide = lat_rim(lon_rim(tangent_coefs[0], 2))
    forward_image = propagate(search_incr, coeff_wide, forward_step)
    backward_image = propagate(search_dual, coeff_wide, adjoint_step)
    earlier = shifted(forward_image[None].astype(jnp.bfloat16), "win", 1).astype(jnp.float32)
    following = shifted(backward_image[None].astype(jnp.bfloat16), "win", -1).astype(jnp.float32)
    covar = localize(ensemble[0], search_dual[0], loc_cols, loc_vals)[None]
    image_dual = covar + search_incr - earlier
    image_obs = obs_var * search_obs + obs_weight * search_incr
    image_incr = search_dual - following + obs_weight * search_obs
    resid_local = (
        jnp.sum(resid_dual * resid_dual)
        + jnp.sum(resid_obs * resid_obs)
        + jnp.sum(resid_incr * resid_incr)
    )
    search_local = (
        jnp.sum(search_dual * search_dual)
        + jnp.sum(search_obs * search_obs)
        + jnp.sum(search_incr * search_incr)
    )
    resid_sq, search_sq = lax.psum((resid_local, search_local), ("win", "lon", "lat"))
    alpha = resid_sq / (search_sq + 1e-06)
    return (
        dual_state + alpha * search_dual,
        dual_obs + alpha * search_obs,
        increment + alpha * search_incr,
        resid_dual - alpha * image_dual,
        resid_obs - alpha * image_obs,
        resid_incr - alpha * image_incr,
    )


def solution(mesh):
    placed = (
        P("win", None, "lat", "lon"),
        P("win", None, "lat", "lon"),
        P("win", None, "lat", "lon"),
        P("win", None, "lat", "lon"),
        P("win", None, "lat", "lon"),
        P("win", None, "lat", "lon"),
        P("win", None, "lat", "lon"),
        P("win", None, "lat", "lon"),
        P("win", None, "lat", "lon"),
        P("win", None, None, "lat", "lon"),
        P("win", None, None, "lat", "lon"),
        P("win", None, "lat", "lon"),
        P("win", None, "lat", "lon"),
        P("lon", None),
        P("lon", None, None, None),
    )
    return jax.shard_map(
        local,
        mesh=mesh,
        in_specs=placed,
        out_specs=(
            P("win", None, "lat", "lon"),
            P("win", None, "lat", "lon"),
            P("win", None, "lat", "lon"),
            P("win", None, "lat", "lon"),
            P("win", None, "lat", "lon"),
            P("win", None, "lat", "lon"),
        ),
        check_vma=False,
    )
```

profile of v0, /device:TPU:0, one launch (start us, length us, event | category | flops | bytes accessed | tf_op | source)
XLA Modules:
  0.0 246.0 jit_solution(6846473304779335088)
XLA Ops:
  0.7 1.6 multiply_reduce_fusion
  2.3 1.4 multiply_reduce_fusion.3
  3.7 1.4 multiply_reduce_fusion.1
  7.1 1.5 multiply_reduce_fusion.4
  10.5 42.0 %all-reduce = (f32[]{:T(128)}, f32[]{:T(128)}) all-reduce(f32[]{:T(128)S(6)} %add.184, f32[]{:T(128)S(6)} %add.186), channel_id=1, replica_groups=mesh['win'=2,'lon'=8,'lat'=2] {'win','lon','lat'}, use_global_device_ids=true, to_apply=%region_3.4 | all-reduce | flops 2 | bytes 16 | tf_op jit(solution)/shard_map/psum | solution.py:137
  54.6 2.5 fusion.14
  57.1 3.9 %collective-permute-start = (bf16[1024,512]{1,0:T(8,128)(2,1)}, bf16[1024,512]{1,0:T(8,128)(2,1)}, u32[]{:S(2)}, u32[]{:S(2)}) collective-permute-start(bf16[1024,512]{1,0:T(8,128)(2,1)} %fusion.14), channel_id=1, source_target_pairs={{2,0},{4,2},{6,4},{8,6},{10,8},{12,10},{14,12},{0,14},{3,1},{5,3},... | collective-permute-start | bytes 3145736 | tf_op jit(solution)/shard_map/ppermute | solution.py:25
  61.1 4.7 %collective-permute-start.16 = (f32[1,16,1,1]{3,1,2,0:T(8,128)S(1)}, f32[1,16,1,1]{3,1,2,0:T(8,128)S(1)}, u32[]{:S(2)}, u32[]{:S(2)}) collective-permute-start(f32[1,16,1,1]{3,1,2,0:T(8,128)S(1)} %get-tuple-element.28), channel_id=1, source_target_pairs={{2,0},{4,2},{6,4},{8,6},{10,8},{12,10},{14,12},{0,14},{3,1},{5,3},... | collective-permute-start | bytes 200 | tf_op jit(solution)/shard_map/ppermute | solution.py:17
  65.9 4.7 %collective-permute-start.20 = (f32[5,16,1,2]{3,1,2,0:T(8,128)S(1)}, f32[5,16,1,2]{3,1,2,0:T(8,128)S(1)}, u32[]{:S(2)}, u32[]{:S(2)}) collective-permute-start(f32[5,16,1,2]{3,1,2,0:T(8,128)S(1)} %get-tuple-element.15), channel_id=1, source_target_pairs={{2,0},{4,2},{6,4},{8,6},{10,8},{12,10},{14,12},{0,14},{3,1},{5,3},... | collective-permute-start | bytes 1928 | tf_op jit(solution)/shard_map/ppermute | solution.py:17
  70.7 2.9 %fusion.2 = bf16[1,512,512]{2,0,1:T(2,128)(2,1)} fusion(bf16[5,512,512]{2,1,0:T(8,128)(2,1)S(1)} %bitcast.200, s32[1,5]{1,0:T(1,128)S(1)} %copy-done.19, s32[]{:T(128)S(6)} %select_n.36), kind=kOutput, calls=%fused_computation.2 | convolution fusion | flops 2621445 | bytes 3145752 | tf_op jit(solution)/shard_map/j,jpq->pq/dot_general | solution.py:83
  73.6 2.9 %fusion.6 = bf16[1,512,512]{2,0,1:T(2,128)(2,1)} fusion(bf16[5,512,512]{2,1,0:T(8,128)(2,1)S(1)} %bitcast.202, s32[1,5]{1,0:T(1,128)S(1)} %copy-done.19, s32[]{:T(128)S(6)} %select_n.34), kind=kOutput, calls=%fused_computation.6 | convolution fusion | flops 2621445 | bytes 3145752 | tf_op jit(solution)/shard_map/j,jpq->pq/dot_general | solution.py:83
  76.6 3.0 %fusion.4 = bf16[1,512,512]{2,0,1:T(2,128)(2,1)} fusion(bf16[5,512,512]{2,1,0:T(8,128)(2,1)S(1)} %bitcast.201, s32[1,5]{1,0:T(1,128)S(1)} %copy-done.19, s32[]{:T(128)S(6)} %select_n.35), kind=kOutput, calls=%fused_computation.4 | convolution fusion | flops 2621445 | bytes 3145752 | tf_op jit(solution)/shard_map/j,jpq->pq/dot_general | solution.py:83
  79.5 2.9 %fusion.10 = bf16[1,512,512]{2,0,1:T(2,128)(2,1)} fusion(bf16[5,512,512]{2,1,0:T(8,128)(2,1)S(1)} %bitcast.204, s32[1,5]{1,0:T(1,128)S(1)} %copy-done.19, s32[]{:T(128)S(6)} %select_n.32), kind=kOutput, calls=%fused_computation.10 | convolution fusion | flops 2621445 | bytes 3145752 | tf_op jit(solution)/shard_map/j,jpq->pq/dot_general | solution.py:83
  82.4 3.0 %fusion.8 = bf16[1,512,512]{2,0,1:T(2,128)(2,1)} fusion(bf16[5,512,512]{2,1,0:T(8,128)(2,1)S(1)} %bitcast.203, s32[1,5]{1,0:T(1,128)S(1)} %copy-done.19, s32[]{:T(128)S(6)} %select_n.33), kind=kOutput, calls=%fused_computation.8 | convolution fusion | flops 2621445 | bytes 3145752 | tf_op jit(solution)/shard_map/j,jpq->pq/dot_general | solution.py:83
  85.4 3.2 %fusion.12 = bf16[1,512,512]{2,0,1:T(2,128)(2,1)} fusion(bf16[5,512,512]{2,1,0:T(8,128)(2,1)S(1)} %bitcast.198, s32[1,5]{1,0:T(1,128)S(1)} %copy-done.19, s32[]{:T(128)S(6)} %select_n.31), kind=kOutput, calls=%fused_computation.12 | convolution fusion | flops 2621445 | bytes 3145752 | tf_op jit(solution)/shard_map/j,jpq->pq/dot_general | solution.py:83
  88.7 2.0 fusion
  90.8 4.7 %collective-permute-start.7 = (f32[1,16,1,1]{3,1,2,0:T(8,128)S(1)}, f32[1,16,1,1]{3,1,2,0:T(8,128)S(1)}, u32[]{:S(2)}, u32[]{:S(2)}) collective-permute-start(f32[1,16,1,1]{3,1,2,0:T(8,128)S(1)} %get-tuple-element.39), channel_id=1, source_target_pairs={{2,0},{4,2},{6,4},{8,6},{10,8},{12,10},{14,12},{0,14},{3,1},{5,3},... | collective-permute-start | bytes 200 | tf_op jit(solution)/shard_map/ppermute | solution.py:17
  95.6 1.5 collective-permute-done.6
  99.9 3.0 %collective-permute-start.8 = (f32[1,16,1,514]{3,1,2,0:T(8,128)S(1)}, f32[1,16,1,514]{3,1,2,0:T(8,128)S(1)}, u32[]{:S(2)}, u32[]{:S(2)}) collective-permute-start(f32[1,16,1,514]{3,1,2,0:T(8,128)S(1)} %pad_maximum_fusion.5), channel_id=1, source_target_pairs={{0,1},{2,3},{4,5},{6,7},{8,9},{10,11},{12,13},{14,15},{16,17},{18,... | collective-permute-start | bytes 98696 | tf_op jit(solution)/shard_map/ppermute | solution.py:16
  104.3 3.0 %collective-permute-start.21 = (f32[5,16,1,516]{3,1,2,0:T(8,128)S(1)}, f32[5,16,1,516]{3,1,2,0:T(8,128)S(1)}, u32[]{:S(2)}, u32[]{:S(2)}) collective-permute-start(f32[5,16,1,516]{3,1,2,0:T(8,128)S(1)} %pad_maximum_fusion.4), channel_id=1, source_target_pairs={{0,1},{2,3},{4,5},{6,7},{8,9},{10,11},{12,13},{14,15},{16,17},{18,... | collective-permute-start | bytes 495368 | tf_op jit(solution)/shard_map/ppermute | solution.py:16
  109.0 1.8 collective-permute-done.22
  111.2 4.7 %collective-permute-start.11 = (f32[1,16,1,1]{3,1,2,0:T(8,128)S(1)}, f32[1,16,1,1]{3,1,2,0:T(8,128)S(1)}, u32[]{:S(2)}, u32[]{:S(2)}) collective-permute-start(f32[1,16,1,1]{3,1,2,0:T(8,128)S(1)} %get-tuple-element.37), channel_id=1, source_target_pairs={{2,0},{4,2},{6,4},{8,6},{10,8},{12,10},{14,12},{0,14},{3,1},{5,3},... | collective-permute-start | bytes 200 | tf_op jit(solution)/shard_map/ppermute | solution.py:17
  116.0 21.8 %collective-permute-done.10 = f32[1,16,1,1]{3,1,2,0:T(8,128)S(1)} collective-permute-done((f32[1,16,1,1]{3,1,2,0:T(8,128)S(1)}, f32[1,16,1,1]{3,1,2,0:T(8,128)S(1)}, u32[]{:S(2)}, u32[]{:S(2)}) %collective-permute-start.10) | collective-permute-done | bytes 96 | tf_op jit(solution)/shard_map/ppermute | solution.py:16
  138.8 1.9 collective-permute-start.12
  142.1 3.0 %collective-permute-start.25 = (f32[1,16,1,514]{3,1,2,0:T(8,128)S(1)}, f32[1,16,1,514]{3,1,2,0:T(8,128)S(1)}, u32[]{:S(2)}, u32[]{:S(2)}) collective-permute-start(f32[1,16,1,514]{3,1,2,0:T(8,128)S(1)} %pad_maximum_fusion.8), channel_id=1, source_target_pairs={{0,1},{2,3},{4,5},{6,7},{8,9},{10,11},{12,13},{14,15},{16,17},{18,... | collective-permute-start | bytes 98696 | tf_op jit(solution)/shard_map/ppermute | solution.py:16
  150.0 1.4 collective-permute-start.27
  151.4 1.9 fusion.16
  156.0 4.5 %collective-permute-start.14 = (bf16[1,16,1,512]{3,1,2,0:T(8,128)(2,1)S(1)}, bf16[1,16,1,512]{3,1,2,0:T(8,128)(2,1)S(1)}, u32[]{:S(2)}, u32[]{:S(2)}) collective-permute-start(bf16[1,16,1,512]{3,1,2,0:T(8,128)(2,1)S(1)} %get-tuple-element.22), channel_id=1, source_target_pairs={{0,16},{1,17},{2,18},{3,19},{4,20},{5,21},{6,22},{7,23},{8,24},{9,... | collective-permute-start | bytes 49160 | tf_op jit(solution)/shard_map/ppermute | solution.py:31
  161.2 33.9 %collective-permute-done.2 = bf16[1024,512]{1,0:T(8,128)(2,1)S(1)} collective-permute-done((bf16[1024,512]{1,0:T(8,128)(2,1)}, bf16[1024,512]{1,0:T(8,128)(2,1)S(1)}, u32[]{:S(2)}, u32[]{:S(2)}) %collective-permute-start.2) | collective-permute-done | bytes 1048608 | tf_op jit(solution)/shard_map/ppermute | solution.py:25
  195.2 1.9 fusion.17
  197.1 2.1 collective-permute-start.5
  201.9 40.9 %collective-permute-done.4 = bf16[1024,512]{1,0:T(8,128)(2,1)S(1)} collective-permute-done((bf16[1024,512]{1,0:T(8,128)(2,1)S(1)}, bf16[1024,512]{1,0:T(8,128)(2,1)S(1)}, u32[]{:S(2)}, u32[]{:S(2)}) %collective-permute-start.4) | collective-permute-done | bytes 1048608 | tf_op jit(solution)/shard_map/ppermute | solution.py:25
  (115 shorter events, 23.6 us)
Async XLA Ops:
  0.6 70.0 %copy-start = (bf16[1,5,512,512]{3,2,1,0:T(8,128)(2,1)S(1)}, bf16[1,5,512,512]{3,2,1,0:T(8,128)(2,1)}, u32[]{:S(2)}) copy-start(bf16[1,5,512,512]{3,2,1,0:T(8,128)(2,1)} %param.29) | copy-start | bytes 7864324
  0.6 65.2 %copy-start.8 = (f32[1,5,16,1,512]{4,3,2,1,0:T(1,128)S(1)}, f32[1,5,16,1,512]{4,3,2,1,0:T(1,128)}, u32[]{:S(2)}) copy-start(f32[1,5,16,1,512]{4,3,2,1,0:T(1,128)} %param.25) | copy-start | bytes 491524
  0.7 70.0 %copy-start.19 = (s32[1,5]{1,0:T(1,128)S(1)}, s32[1,5]{1,0:T(1,128)}, u32[]{:S(2)}) copy-start(s32[1,5]{1,0:T(1,128)} %param.28) | copy-start | bytes 64
  57.1 89.4 %collective-permute-start = (bf16[1024,512]{1,0:T(8,128)(2,1)}, bf16[1024,512]{1,0:T(8,128)(2,1)}, u32[]{:S(2)}, u32[]{:S(2)}) collective-permute-start(bf16[1024,512]{1,0:T(8,128)(2,1)} %fusion.14), channel_id=1, source_target_pairs={{2,0},{4,2},{6,4},{8,6},{10,8},{12,10},{14,12},{0,14},{3,1},{5,3},... | collective-permute-start | bytes 3145736 | tf_op jit(solution)/shard_map/ppermute | solution.py:25
  61.1 29.7 %collective-permute-start.15 = (f32[1,16,1,1]{3,1,2,0:T(8,128)S(1)}, f32[1,16,1,1]{3,1,2,0:T(8,128)S(1)}, u32[]{:S(2)}, u32[]{:S(2)}) collective-permute-start(f32[1,16,1,1]{3,1,2,0:T(8,128)S(1)} %get-tuple-element.27), channel_id=1, source_target_pairs={{0,2},{2,4},{4,6},{6,8},{8,10},{10,12},{12,14},{14,0},{1,3},{3,5},... | collective-permute-start | bytes 200 | tf_op jit(solution)/shard_map/ppermute | solution.py:16
  61.1 29.8 %collective-permute-start.16 = (f32[1,16,1,1]{3,1,2,0:T(8,128)S(1)}, f32[1,16,1,1]{3,1,2,0:T(8,128)S(1)}, u32[]{:S(2)}, u32[]{:S(2)}) collective-permute-start(f32[1,16,1,1]{3,1,2,0:T(8,128)S(1)} %get-tuple-element.28), channel_id=1, source_target_pairs={{2,0},{4,2},{6,4},{8,6},{10,8},{12,10},{14,12},{0,14},{3,1},{5,3},... | collective-permute-start | bytes 200 | tf_op jit(solution)/shard_map/ppermute | solution.py:17
  65.9 34.0 %collective-permute-start.19 = (f32[5,16,1,2]{3,1,2,0:T(8,128)S(1)}, f32[5,16,1,2]{3,1,2,0:T(8,128)S(1)}, u32[]{:S(2)}, u32[]{:S(2)}) collective-permute-start(f32[5,16,1,2]{3,1,2,0:T(8,128)S(1)} %get-tuple-element.14), channel_id=1, source_target_pairs={{0,2},{2,4},{4,6},{6,8},{8,10},{10,12},{12,14},{14,0},{1,3},{3,5},... | collective-permute-start | bytes 1928 | tf_op jit(solution)/shard_map/ppermute | solution.py:16
  65.9 37.0 %collective-permute-start.20 = (f32[5,16,1,2]{3,1,2,0:T(8,128)S(1)}, f32[5,16,1,2]{3,1,2,0:T(8,128)S(1)}, u32[]{:S(2)}, u32[]{:S(2)}) collective-permute-start(f32[5,16,1,2]{3,1,2,0:T(8,128)S(1)} %get-tuple-element.15), channel_id=1, source_target_pairs={{2,0},{4,2},{6,4},{8,6},{10,8},{12,10},{14,12},{0,14},{3,1},{5,3},... | collective-permute-start | bytes 1928 | tf_op jit(solution)/shard_map/ppermute | solution.py:17
  90.8 6.4 %collective-permute-start.6 = (f32[1,16,1,1]{3,1,2,0:T(8,128)S(1)}, f32[1,16,1,1]{3,1,2,0:T(8,128)S(1)}, u32[]{:S(2)}, u32[]{:S(2)}) collective-permute-start(f32[1,16,1,1]{3,1,2,0:T(8,128)S(1)} %get-tuple-element.38), channel_id=1, source_target_pairs={{0,2},{2,4},{4,6},{6,8},{8,10},{10,12},{12,14},{14,0},{1,3},{3,5},... | collective-permute-start | bytes 200 | tf_op jit(solution)/shard_map/ppermute | solution.py:16
  90.8 7.6 %collective-permute-start.7 = (f32[1,16,1,1]{3,1,2,0:T(8,128)S(1)}, f32[1,16,1,1]{3,1,2,0:T(8,128)S(1)}, u32[]{:S(2)}, u32[]{:S(2)}) collective-permute-start(f32[1,16,1,1]{3,1,2,0:T(8,128)S(1)} %get-tuple-element.39), channel_id=1, source_target_pairs={{2,0},{4,2},{6,4},{8,6},{10,8},{12,10},{14,12},{0,14},{3,1},{5,3},... | collective-permute-start | bytes 200 | tf_op jit(solution)/shard_map/ppermute | solution.py:17
  97.2 7.2 %collective-permute-start.17 = (f32[1,16,1,514]{3,1,2,0:T(8,128)S(1)}, f32[1,16,1,514]{3,1,2,0:T(8,128)S(1)}, u32[]{:S(2)}, u32[]{:S(2)}) collective-permute-start(f32[1,16,1,514]{3,1,2,0:T(8,128)S(1)} %pad_maximum_fusion.7), channel_id=1, source_target_pairs={{0,1},{2,3},{4,5},{6,7},{8,9},{10,11},{12,13},{14,15},{16,17},{18,... | collective-permute-start | bytes 98696 | tf_op jit(solution)/shard_map/ppermute | solution.py:16
  98.5 8.9 %collective-permute-start.18 = (f32[1,16,1,514]{3,1,2,0:T(8,128)S(1)}, f32[1,16,1,514]{3,1,2,0:T(8,128)S(1)}, u32[]{:S(2)}, u32[]{:S(2)}) collective-permute-start(f32[1,16,1,514]{3,1,2,0:T(8,128)S(1)} %pad_maximum_fusion.7), channel_id=1, source_target_pairs={{1,0},{3,2},{5,4},{7,6},{9,8},{11,10},{13,12},{15,14},{17,16},{19,... | collective-permute-start | bytes 98696 | tf_op jit(solution)/shard_map/ppermute | solution.py:17
  99.9 8.9 %collective-permute-start.8 = (f32[1,16,1,514]{3,1,2,0:T(8,128)S(1)}, f32[1,16,1,514]{3,1,2,0:T(8,128)S(1)}, u32[]{:S(2)}, u32[]{:S(2)}) collective-permute-start(f32[1,16,1,514]{3,1,2,0:T(8,128)S(1)} %pad_maximum_fusion.5), channel_id=1, source_target_pairs={{0,1},{2,3},{4,5},{6,7},{8,9},{10,11},{12,13},{14,15},{16,17},{18,... | collective-permute-start | bytes 98696 | tf_op jit(solution)/shard_map/ppermute | solution.py:16
  102.9 6.0 %collective-permute-start.9 = (f32[1,16,1,514]{3,1,2,0:T(8,128)S(1)}, f32[1,16,1,514]{3,1,2,0:T(8,128)S(1)}, u32[]{:S(2)}, u32[]{:S(2)}) collective-permute-start(f32[1,16,1,514]{3,1,2,0:T(8,128)S(1)} %pad_maximum_fusion.5), channel_id=1, source_target_pairs={{1,0},{3,2},{5,4},{7,6},{9,8},{11,10},{13,12},{15,14},{17,16},{19,... | collective-permute-start | bytes 98696 | tf_op jit(solution)/shard_map/ppermute | solution.py:17
  104.3 4.6 %collective-permute-start.21 = (f32[5,16,1,516]{3,1,2,0:T(8,128)S(1)}, f32[5,16,1,516]{3,1,2,0:T(8,128)S(1)}, u32[]{:S(2)}, u32[]{:S(2)}) collective-permute-start(f32[5,16,1,516]{3,1,2,0:T(8,128)S(1)} %pad_maximum_fusion.4), channel_id=1, source_target_pairs={{0,1},{2,3},{4,5},{6,7},{8,9},{10,11},{12,13},{14,15},{16,17},{18,... | collective-permute-start | bytes 495368 | tf_op jit(solution)/shard_map/ppermute | solution.py:16
  107.4 3.3 %collective-permute-start.22 = (f32[5,16,1,516]{3,1,2,0:T(8,128)S(1)}, f32[5,16,1,516]{3,1,2,0:T(8,128)S(1)}, u32[]{:S(2)}, u32[]{:S(2)}) collective-permute-start(f32[5,16,1,516]{3,1,2,0:T(8,128)S(1)} %pad_maximum_fusion.4), channel_id=1, source_target_pairs={{1,0},{3,2},{5,4},{7,6},{9,8},{11,10},{13,12},{15,14},{17,16},{19,... | collective-permute-start | bytes 495368 | tf_op jit(solution)/shard_map/ppermute | solution.py:17
  108.8 39.8 %collective-permute-start.1 = (bf16[1024,512]{1,0:T(8,128)(2,1)}, bf16[1024,512]{1,0:T(8,128)(2,1)S(1)}, u32[]{:S(2)}, u32[]{:S(2)}) collective-permute-start(bf16[1024,512]{1,0:T(8,128)(2,1)} %fusion.14), channel_id=1, source_target_pairs={{14,0},{0,2},{2,4},{4,6},{6,8},{8,10},{10,12},{12,14},{15,1},{1,3}... | collective-permute-start | bytes 3145736 | tf_op jit(solution)/shard_map/ppermute | solution.py:25
  111.2 26.6 %collective-permute-start.10 = (f32[1,16,1,1]{3,1,2,0:T(8,128)S(1)}, f32[1,16,1,1]{3,1,2,0:T(8,128)S(1)}, u32[]{:S(2)}, u32[]{:S(2)}) collective-permute-start(f32[1,16,1,1]{3,1,2,0:T(8,128)S(1)} %get-tuple-element.36), channel_id=1, source_target_pairs={{0,2},{2,4},{4,6},{6,8},{8,10},{10,12},{12,14},{14,0},{1,3},{3,5},... | collective-permute-start | bytes 200 | tf_op jit(solution)/shard_map/ppermute | solution.py:16
  111.2 27.5 %collective-permute-start.11 = (f32[1,16,1,1]{3,1,2,0:T(8,128)S(1)}, f32[1,16,1,1]{3,1,2,0:T(8,128)S(1)}, u32[]{:S(2)}, u32[]{:S(2)}) collective-permute-start(f32[1,16,1,1]{3,1,2,0:T(8,128)S(1)} %get-tuple-element.37), channel_id=1, source_target_pairs={{2,0},{4,2},{6,4},{8,6},{10,8},{12,10},{14,12},{0,14},{3,1},{5,3},... | collective-permute-start | bytes 200 | tf_op jit(solution)/shard_map/ppermute | solution.py:17
  116.0 24.7 %collective-permute-start.23 = (f32[1,16,1,1]{3,1,2,0:T(8,128)S(1)}, f32[1,16,1,1]{3,1,2,0:T(8,128)S(1)}, u32[]{:S(2)}, u32[]{:S(2)}) collective-permute-start(f32[1,16,1,1]{3,1,2,0:T(8,128)S(1)} %get-tuple-element.23), channel_id=1, source_target_pairs={{0,2},{2,4},{4,6},{6,8},{8,10},{10,12},{12,14},{14,0},{1,3},{3,5},... | collective-permute-start | bytes 200 | tf_op jit(solution)/shard_map/ppermute | solution.py:16
  137.8 4.2 %collective-permute-start.24 = (f32[1,16,1,1]{3,1,2,0:T(8,128)S(1)}, f32[1,16,1,1]{3,1,2,0:T(8,128)S(1)}, u32[]{:S(2)}, u32[]{:S(2)}) collective-permute-start(f32[1,16,1,1]{3,1,2,0:T(8,128)S(1)} %get-tuple-element.24), channel_id=1, source_target_pairs={{2,0},{4,2},{6,4},{8,6},{10,8},{12,10},{14,12},{0,14},{3,1},{5,3},... | collective-permute-start | bytes 200 | tf_op jit(solution)/shard_map/ppermute | solution.py:17
  138.8 6.4 %collective-permute-start.12 = (f32[1,16,1,514]{3,1,2,0:T(8,128)S(1)}, f32[1,16,1,514]{3,1,2,0:T(8,128)S(1)}, u32[]{:S(2)}, u32[]{:S(2)}) collective-permute-start(f32[1,16,1,514]{3,1,2,0:T(8,128)S(1)} %pad_maximum_fusion.6), channel_id=1, source_target_pairs={{0,1},{2,3},{4,5},{6,7},{8,9},{10,11},{12,13},{14,15},{16,17},{18,... | collective-permute-start | bytes 98696 | tf_op jit(solution)/shard_map/ppermute | solution.py:16
  140.7 5.7 %collective-permute-start.13 = (f32[1,16,1,514]{3,1,2,0:T(8,128)S(1)}, f32[1,16,1,514]{3,1,2,0:T(8,128)S(1)}, u32[]{:S(2)}, u32[]{:S(2)}) collective-permute-start(f32[1,16,1,514]{3,1,2,0:T(8,128)S(1)} %pad_maximum_fusion.6), channel_id=1, source_target_pairs={{1,0},{3,2},{5,4},{7,6},{9,8},{11,10},{13,12},{15,14},{17,16},{19,... | collective-permute-start | bytes 98696 | tf_op jit(solution)/shard_map/ppermute | solution.py:17
  142.1 5.8 %collective-permute-start.25 = (f32[1,16,1,514]{3,1,2,0:T(8,128)S(1)}, f32[1,16,1,514]{3,1,2,0:T(8,128)S(1)}, u32[]{:S(2)}, u32[]{:S(2)}) collective-permute-start(f32[1,16,1,514]{3,1,2,0:T(8,128)S(1)} %pad_maximum_fusion.8), channel_id=1, source_target_pairs={{0,1},{2,3},{4,5},{6,7},{8,9},{10,11},{12,13},{14,15},{16,17},{18,... | collective-permute-start | bytes 98696 | tf_op jit(solution)/shard_map/ppermute | solution.py:16
  145.1 3.1 %collective-permute-start.26 = (f32[1,16,1,514]{3,1,2,0:T(8,128)S(1)}, f32[1,16,1,514]{3,1,2,0:T(8,128)S(1)}, u32[]{:S(2)}, u32[]{:S(2)}) collective-permute-start(f32[1,16,1,514]{3,1,2,0:T(8,128)S(1)} %pad_maximum_fusion.8), channel_id=1, source_target_pairs={{1,0},{3,2},{5,4},{7,6},{9,8},{11,10},{13,12},{15,14},{17,16},{19,... | collective-permute-start | bytes 98696 | tf_op jit(solution)/shard_map/ppermute | solution.py:17
  146.5 48.6 %collective-permute-start.2 = (bf16[1024,512]{1,0:T(8,128)(2,1)}, bf16[1024,512]{1,0:T(8,128)(2,1)S(1)}, u32[]{:S(2)}, u32[]{:S(2)}) collective-permute-start(bf16[1024,512]{1,0:T(8,128)(2,1)} %collective-permute-done), channel_id=1, source_target_pairs={{2,0},{4,2},{6,4},{8,6},{10,8},{12,10},{14,12},{0,14},{3,1},{5,3},... | collective-permute-start | bytes 3145736 | tf_op jit(solution)/shard_map/ppermute | solution.py:25
  148.6 48.5 %collective-permute-start.3 = (bf16[1024,512]{1,0:T(8,128)(2,1)S(1)}, bf16[1024,512]{1,0:T(8,128)(2,1)S(1)}, u32[]{:S(2)}, u32[]{:S(2)}) collective-permute-start(bf16[1024,512]{1,0:T(8,128)(2,1)S(1)} %collective-permute-done.1), channel_id=1, source_target_pairs={{14,0},{0,2},{2,4},{4,6},{6,8},{8,10},{10,12},{12,14},{15,1},{1,3}... | collective-permute-start | bytes 3145736 | tf_op jit(solution)/shard_map/ppermute | solution.py:25
  150.0 10.5 %collective-permute-start.27 = (bf16[1,16,1,512]{3,2,1,0:T(2,128)(2,1)S(1)}, bf16[1,16,1,512]{3,2,1,0:T(2,128)(2,1)S(1)}, u32[]{:S(2)}, u32[]{:S(2)}) collective-permute-start(bf16[1,16,1,512]{3,2,1,0:T(2,128)(2,1)S(1)} %convert_element_type.106), channel_id=1, source_target_pairs={{16,0},{17,1},{18,2},{19,3},{20,4},{21,5},{22,6},{23,7},{24,8},{25... | collective-permute-start | bytes 49160 | tf_op jit(solution)/shard_map/ppermute | solution.py:31
  153.4 45.8 %copy-start.6 = (bf16[1,512,512]{2,0,1:T(2,128)(2,1)S(1)}, bf16[1,512,512]{2,0,1:T(2,128)(2,1)}, u32[]{:S(2)}) copy-start(bf16[1,512,512]{2,0,1:T(2,128)(2,1)} %fusion.8) | copy-start | bytes 1572868
  156.0 89.2 %collective-permute-start.14 = (bf16[1,16,1,512]{3,1,2,0:T(8,128)(2,1)S(1)}, bf16[1,16,1,512]{3,1,2,0:T(8,128)(2,1)S(1)}, u32[]{:S(2)}, u32[]{:S(2)}) collective-permute-start(bf16[1,16,1,512]{3,1,2,0:T(8,128)(2,1)S(1)} %get-tuple-element.22), channel_id=1, source_target_pairs={{0,16},{1,17},{2,18},{3,19},{4,20},{5,21},{6,22},{7,23},{8,24},{9,... | collective-permute-start | bytes 49160 | tf_op jit(solution)/shard_map/ppermute | solution.py:31
  195.1 47.6 %collective-permute-start.4 = (bf16[1024,512]{1,0:T(8,128)(2,1)S(1)}, bf16[1024,512]{1,0:T(8,128)(2,1)S(1)}, u32[]{:S(2)}, u32[]{:S(2)}) collective-permute-start(bf16[1024,512]{1,0:T(8,128)(2,1)S(1)} %collective-permute-done.2), channel_id=1, source_target_pairs={{2,0},{4,2},{6,4},{8,6},{10,8},{12,10},{14,12},{0,14},{3,1},{5,3},... | collective-permute-start | bytes 3145736 | tf_op jit(solution)/shard_map/ppermute | solution.py:25
  197.1 46.4 %collective-permute-start.5 = (bf16[1024,512]{1,0:T(8,128)(2,1)S(1)}, bf16[1024,512]{1,0:T(8,128)(2,1)S(1)}, u32[]{:S(2)}, u32[]{:S(2)}) collective-permute-start(bf16[1024,512]{1,0:T(8,128)(2,1)S(1)} %collective-permute-done.3), channel_id=1, source_target_pairs={{14,0},{0,2},{2,4},{4,6},{6,8},{8,10},{10,12},{12,14},{15,1},{1,3}... | collective-permute-start | bytes 3145736 | tf_op jit(solution)/shard_map/ppermute | solution.py:25
  (16 other events, 170.9 us)
where the time goes:
time: 247 us; the launch traced here: 246 us
  waiting for transfers between devices  100 us (40%)
  starting transfers between devices  53 us (21%)
  blocking collectives  42 us (17%)
  matrix products  27.6 us (11%)
  other arithmetic  11.9 us (5%)
  between operations  6.45 us (3%)
  local copies, waits for them, and re-layouts  4.66 us (2%)
    ppermute x6, waiting for transfers between devices, passed_along(): return lax.ppermute(block, axis, route)  74.9 us
    psum x1, blocking collectives, local(): lax.psum((resid_local, search_local), ('win', 'lon', 'lat'))  42 us
    ppermute x10, starting transfers between devices, extended_2(): after = lax.ppermute(leading, axis, down)  26.2 us
    ppermute x10, waiting for transfers between devices, extended_2(): before = lax.ppermute(last, axis, up)  23.3 us
    dot_general x7, matrix products, weight_for(): jnp.einsum('j,jpq->pq', match, tiles, preferred_element_type=jnp.float32)  19.9 us
    ppermute x10, starting transfers between devices, extended_2(): before = lax.ppermute(last, axis, up)  12.3 us
    ppermute x6, starting transfers between devices, passed_along(): return lax.ppermute(block, axis, route)  8.56 us
    ppermute x2, starting transfers between devices, shifted(): lax.ppermute(value, axis, [(source, source + steps) for source in range(l...  5.96 us
  transfers between devices with their start and end apart: 28, of which 6 were waited for; matrix products, arithmetic and copies ran while one was open for 14% of the time, Pallas kernels for 0%

commit v1 on v0

v1 whole, which is shorter than its diff:
```python
import functools

import jax
import jax.numpy as jnp
from jax import lax
from jax.experimental import pallas as pl
from jax.experimental.pallas import tpu as pltpu
from jax.sharding import PartitionSpec as P

REACH = 3
CHUNKS = 8
LAG = 2
LANES = 128
MESH = pl.DeviceIdType.MESH
BF16 = jnp.bfloat16
F32 = jnp.float32


def remote(src, dst, send, recv, where):
    return pltpu.make_async_remote_copy(
        src_ref=src,
        dst_ref=dst,
        send_sem=send,
        recv_sem=recv,
        device_id=where,
        device_id_type=MESH,
    )


def kernel(
    sizes,
    dual_state, dual_obs, increment,
    resid_dual, resid_obs, resid_incr,
    search_dual, search_obs, search_incr,
    ens, coefs, obs_weight, obs_var, cols, vals,
    next_dual, next_obs, next_incr,
    next_res_dual, next_res_obs, next_res_incr,
    near, near_s, own_s, w_home, w_out, w_in,
    g_own, g_lat, g_left, g_right,
    part, part_lon, pair, part_col,
    moved, moved_in, acc, back, covar_flat,
    e_send, e_recv, s_send, s_recv, w_send, w_recv, f_send, f_recv,
    g_send, g_recv, a_send, a_recv, b_send, b_recv,
    m_send, m_recv, r_send, r_recv,
):
    wins, bands, lats, members, levels, block = sizes
    colors = wins * lats
    pieces = block // LANES
    rows = members * levels // CHUNKS
    group = rows // levels
    share = block // colors
    win = lax.axis_index("win")
    lon = lax.axis_index("lon")
    lat = lax.axis_index("lat")
    color = win * lats + lat

    def at(lon_step=0, other_lat=False, win_step=0):
        return {
            "win": lax.rem(win + win_step + wins, wins),
            "lon": lax.rem(lon + lon_step + bands, bands),
            "lat": 1 - lat if other_lat else lat,
        }

    def peer(step):
        index = lax.rem(color + step, colors)
        return index, {"win": index // lats, "lon": lon, "lat": lax.rem(index, lats)}

    barrier = pltpu.get_barrier_semaphore()
    greeted = [at(step) for step in range(1, bands)]
    greeted += [peer(step)[1] for step in range(1, colors)]
    greeted += [at(1, True), at(-1, True)]
    for where in greeted:
        pl.semaphore_signal(barrier, inc=1, device_id=where, device_id_type=MESH)

    def rows_of(ref, base):
        return [ref[pl.ds(base + j, levels, stride=pieces), :] for j in range(pieces)]

    flat = levels * pieces
    for j, (u, v) in enumerate(zip(rows_of(search_dual, 0), rows_of(search_incr, 0))):
        own_s[:, pl.ds(j * LANES, LANES)] = u
        g_own[0, :, pl.ds(j * LANES, LANES)] = v
        g_own[1, :, pl.ds(j * LANES, LANES)] = u
    for c in range(5):
        for j, value in enumerate(rows_of(coefs, c * flat)):
            g_own[2 + c, :, pl.ds(j * LANES, LANES)] = value

    resid_sq = jnp.sum(resid_dual[...] ** 2 + resid_obs[...] ** 2 + resid_incr[...] ** 2)
    search_sq = jnp.sum(search_dual[...] ** 2 + search_obs[...] ** 2 + search_incr[...] ** 2)
    first_row = lax.broadcasted_iota(jnp.int32, (8, LANES), 0) == 0
    part[...] = jnp.where(first_row, resid_sq, search_sq)
    part_lon[lon] = part[...]

    def slot_of(step):
        target = lax.rem(lon + step + bands, bands)
        slot = jnp.int32(0)
        found = jnp.int32(0)
        for j in range(vals.shape[0]):
            hit = cols[0, j] == target
            slot = jnp.where(hit, j, slot)
            found = jnp.where(hit, 1, found)
        return slot, found > 0

    mine = pl.ds(pl.multiple_of(color * share, share), share)
    for d in range(1, REACH + 1):
        slot, found = slot_of(d)
        w_out[d - 1] = jnp.where(found, vals[slot, mine, :], jnp.zeros((share, block), BF16))

    pl.semaphore_wait(barrier, len(greeted))

    started = []

    def go(copy):
        copy.start()
        started.append(copy)

    for d in range(1, REACH + 1):
        go(remote(own_s, near_s.at[d - 1], s_send.at[d - 1], s_recv.at[d - 1], at(d)))
    for step in range(1, bands):
        go(remote(part, part_lon.at[lon], a_send.at[step], a_recv.at[lon], at(step)))
    go(remote(g_own, g_lat, g_send.at[0], g_recv.at[0], at(0, True)))
    head = g_own.at[:, :, pl.ds(0, LANES)]
    tail = g_own.at[:, :, pl.ds(block - LANES, LANES)]
    for other in range(2):
        go(remote(tail, g_left.at[other], g_send.at[1 + other], g_recv.at[1 + other], at(1, other == 1)))
        go(remote(head, g_right.at[other], g_send.at[3 + other], g_recv.at[3 + other], at(-1, other == 1)))
    for d in range(1, REACH + 1):
        go(remote(w_out.at[d - 1], w_in.at[d - 1, mine], w_send.at[d - 1], w_recv.at[d - 1], at(d)))

    even = lax.rem(lon, 2) == 0

    def lines(t):
        return pl.ds(pl.multiple_of(t * rows, rows), rows)

    def two_on(t):
        return remote(ens.at[lines(t)], near.at[1, lines(t)], e_send.at[0, t], e_recv.at[0, t], at(2))

    def one_on_even(t):
        return remote(ens.at[lines(t)], near.at[0, lines(t)], e_send.at[1, t], e_recv.at[1, t], at(1))

    def one_on_odd(t):
        return remote(near.at[1, lines(t)], near.at[0, lines(t)], e_send.at[1, t], e_recv.at[1, t], at(-1))

    def three_on(t):
        return remote(near.at[0, lines(t)], near.at[2, lines(t)], e_send.at[2, t], e_recv.at[2, t], at(2))

    def first_sends(t, carry):
        two_on(t).start()

        @pl.when(even)
        def _():
            one_on_even(t).start()

        return carry

    lax.fori_loop(0, CHUNKS, first_sends, 0)

    for d in range(REACH + 1):
        slot, found = slot_of(-d)
        w_home[d] = jnp.where(found, vals[slot], jnp.zeros((block, block), BF16))
    acc[...] = jnp.zeros_like(acc)

    for step in range(1, bands):
        source = lax.rem(lon + step, bands)
        remote(part, part_lon.at[source], a_send.at[step], a_recv.at[source], at(0)).wait_recv()
    pair[...] = jnp.sum(part_lon[...], axis=0)
    part_col[color] = pair[...]
    for step in range(1, colors):
        _, where = peer(step)
        go(remote(pair, part_col.at[color], b_send.at[step], b_recv.at[color], where))

    remote(g_own, g_lat, g_send.at[0], g_recv.at[0], at(0)).wait_recv()
    for other in range(2):
        remote(tail, g_left.at[other], g_send.at[1 + other], g_recv.at[1 + other], at(0)).wait_recv()
        remote(head, g_right.at[other], g_send.at[3 + other], g_recv.at[3 + other], at(0)).wait_recv()

    def wide(k, other):
        middle = g_lat if other else g_own
        return jnp.concatenate([g_left[other, k], middle[k], g_right[other, k]], axis=1)

    span = block + 2 * LANES

    def east(x):
        return pltpu.roll(x, span - 1, 1)

    def west(x):
        return pltpu.roll(x, 1, 1)

    here = [wide(k, 0) for k in range(7)]
    over = [wide(k, 1) for k in range(7)]
    south_row = lat == 0
    cross = jnp.where(south_row, here[5], here[6])
    cross_over = jnp.where(south_row, over[6], over[5])

    def forward(v, beyond, c, between):
        return (0.5 + c[2]) * v + c[3] * east(v) + c[4] * west(v) + between * beyond

    def adjoint(u, beyond, c, between):
        return (0.5 + c[2]) * u + west(c[3] * u) + east(c[4] * u) + between * beyond

    once = forward(here[0], over[0], here, cross)
    once_over = forward(over[0], here[0], over, cross_over)
    twice = forward(once, once_over, here, cross)
    back_once = adjoint(here[1], over[1], here, cross_over)
    back_over = adjoint(over[1], here[1], over, cross)
    back_twice = adjoint(back_once, back_over, here, cross_over)
    for j in range(pieces):
        cut = slice((j + 1) * LANES, (j + 2) * LANES)
        moved[0, pl.ds(j, levels, stride=pieces), :] = twice[:, cut]
        moved[1, pl.ds(j, levels, stride=pieces), :] = back_twice[:, cut]
    for k, way in enumerate((1, -1)):
        go(remote(moved.at[k], moved_in.at[k], m_send.at[k], m_recv.at[k], at(0, False, way)))

    for d in range(1, REACH + 1):
        part_of = w_in.at[d - 1, mine]
        remote(w_out.at[d - 1], part_of, w_send.at[d - 1], w_recv.at[d - 1], at(0)).wait_recv()
        for step in range(1, colors):
            _, where = peer(step)
            go(remote(part_of, part_of, f_send.at[step, d - 1], f_recv.at[color, d - 1], where))
    for d in range(1, REACH + 1):
        remote(own_s, near_s.at[d - 1], s_send.at[d - 1], s_recv.at[d - 1], at(0)).wait_recv()

    def shares_in():
        for d in range(1, REACH + 1):
            for step in range(1, colors):
                source, where = peer(step)
                theirs = pl.ds(pl.multiple_of(source * share, share), share)
                spot = w_in.at[d - 1, theirs]
                remote(spot, spot, f_send.at[step, d - 1], f_recv.at[source, d - 1], where).wait_recv()

    def spread_of(t):
        def read(ref, search):
            member = ref[...].astype(F32).reshape(group, levels, block)
            product = (member * search[None]).astype(BF16).reshape(rows, block)
            return member, product

        def weigh(member, spread):
            return jnp.sum(member * spread.reshape(group, levels, block), axis=0)

        member, product = read(ens.at[lines(t)], own_s[...])
        total = jnp.dot(product, w_home[0], preferred_element_type=F32)
        for d in range(1, REACH + 1):
            far, far_product = read(near.at[d - 1, lines(t)], near_s[d - 1])
            total = total + jnp.dot(far_product, w_home[d], preferred_element_type=F32)
            acc[d] += weigh(far, jnp.dot(product, w_in[d - 1], preferred_element_type=F32))
        acc[0] += weigh(member, total)

    def step_of(t, carry):
        @pl.when(t < CHUNKS)
        def _():
            two_on(t).wait_recv()

            @pl.when(jnp.logical_not(even))
            def _():
                one_on_odd(t).start()

            one_on_even(t).wait_recv()
            three_on(t).start()

        @pl.when(t == LAG)
        def _():
            shares_in()

        @pl.when(t >= LAG)
        def _():
            three_on(t - LAG).wait_recv()
            spread_of(t - LAG)

        return carry

    lax.fori_loop(0, CHUNKS + LAG, step_of, 0)

    for d in range(1, REACH + 1):
        go(remote(acc.at[d], back.at[d - 1], r_send.at[d - 1], r_recv.at[d - 1], at(-d)))

    for step in range(1, colors):
        source, where = peer(step)
        remote(pair, part_col.at[source], b_send.at[step], b_recv.at[source], where).wait_recv()
    sums = jnp.sum(part_col[...], axis=0)
    alpha = sums[0:1, :] / (sums[1:2, :] + 1e-6)

    next_dual[...] = dual_state[...] + alpha * search_dual[...]
    next_obs[...] = dual_obs[...] + alpha * search_obs[...]
    next_incr[...] = increment[...] + alpha * search_incr[...]
    image_obs = obs_var[...] * search_obs[...] + obs_weight[...] * search_incr[...]
    next_res_obs[...] = resid_obs[...] - alpha * image_obs
    for k in range(2):
        remote(moved.at[k], moved_in.at[k], m_send.at[k], m_recv.at[k], at(0)).wait_recv()
    later = jnp.where(win < wins - 1, moved_in[1], 0.0)
    image_incr = search_dual[...] - later + obs_weight[...] * search_obs[...]
    next_res_incr[...] = resid_incr[...] - alpha * image_incr
    prior = jnp.where(win > 0, moved_in[0], 0.0)

    for d in range(1, REACH + 1):
        remote(acc.at[d], back.at[d - 1], r_send.at[d - 1], r_recv.at[d - 1], at(0)).wait_recv()
    covar = (acc[0] + back[0] + back[1] + back[2]) / (members - 1)
    for j in range(pieces):
        covar_flat[pl.ds(j, levels, stride=pieces), :] = covar[:, j * LANES:(j + 1) * LANES]
    image_dual = covar_flat[...] + search_incr[...] - prior
    next_res_dual[...] = resid_dual[...] - alpha * image_dual

    for copy in started:
        copy.wait_send()

    def sent(t, carry):
        two_on(t).wait_send()
        one_on_even(t).wait_send()
        three_on(t).wait_send()
        return carry

    lax.fori_loop(0, CHUNKS, sent, 0)


def local(wins, bands, lats, *args):
    fields = list(args)
    _, members, levels, _, block = args[9].shape
    flat = levels * block // LANES
    for k in (0, 1, 2, 3, 4, 5, 6, 7, 8, 11, 12):
        fields[k] = args[k].reshape(flat, LANES)
    fields[9] = args[9].reshape(members * levels, block)
    fields[10] = args[10].reshape(5 * flat, LANES)
    fields[14] = args[14][0]
    colors = wins * lats
    share = block // colors
    vmem = pl.BlockSpec(memory_space=pltpu.VMEM)
    specs = [vmem] * 15
    specs[13] = pl.BlockSpec(memory_space=pltpu.SMEM)
    dma = pltpu.SemaphoreType.DMA
    pairs = [(3, CHUNKS), (REACH,), (REACH,), (colors, REACH), (5,), (bands,), (colors,), (2,), (REACH,)]
    outs = pl.pallas_call(
        functools.partial(kernel, (wins, bands, lats, members, levels, block)),
        out_shape=[jax.ShapeDtypeStruct((flat, LANES), F32)] * 6,
        in_specs=specs,
        out_specs=[vmem] * 6,
        scratch_shapes=[
            pltpu.VMEM((REACH, members * levels, block), BF16),
            pltpu.VMEM((REACH, levels, block), F32),
            pltpu.VMEM((levels, block), F32),
            pltpu.VMEM((REACH + 1, block, block), BF16),
            pltpu.VMEM((REACH, share, block), BF16),
            pltpu.VMEM((REACH, block, block), BF16),
            pltpu.VMEM((7, levels, block), F32),
            pltpu.VMEM((7, levels, block), F32),
            pltpu.VMEM((2, 7, levels, LANES), F32),
            pltpu.VMEM((2, 7, levels, LANES), F32),
            pltpu.VMEM((8, LANES), F32),
            pltpu.VMEM((bands, 8, LANES), F32),
            pltpu.VMEM((8, LANES), F32),
            pltpu.VMEM((colors, 8, LANES), F32),
            pltpu.VMEM((2, flat, LANES), F32),
            pltpu.VMEM((2, flat, LANES), F32),
            pltpu.VMEM((REACH + 1, levels, block), F32),
            pltpu.VMEM((REACH, levels, block), F32),
            pltpu.VMEM((flat, LANES), F32),
        ] + [dma(shape) for shape in pairs for _ in range(2)],
        compiler_params=pltpu.CompilerParams(
            collective_id=0, has_side_effects=True, vmem_limit_bytes=40 * 1024 * 1024
        ),
    )(*fields)
    return tuple(out.reshape(args[0].shape) for out in outs)


def solution(mesh):
    wins, bands, lats = (mesh.shape[name] for name in ("win", "lon", "lat"))
    field = P("win", None, "lat", "lon")
    deep = P("win", None, None, "lat", "lon")
    return jax.shard_map(
        functools.partial(local, wins, bands, lats),
        mesh=mesh,
        in_specs=(field,) * 9 + (deep, deep, field, field, P("lon", None), P("lon", None, None, None)),
        out_specs=(field,) * 6,
        check_vma=False,
    )
```

time: 247 us -> 126 us (0.51)
  Pallas kernels: 0 us -> 108 us
  waiting for transfers between devices: 100 us -> 0 us
  starting transfers between devices: 53 us -> 0 us
  blocking collectives: 42 us -> 0 us
  matrix products: 27.6 us -> 0 us
  other arithmetic: 11.9 us -> 0 us
  local copies, waits for them, and re-layouts: 4.66 us -> 16.5 us
  between operations: 6.45 us -> 0.67 us
    pallas_call x0 -> x1, Pallas kernels: none -> 108 us  [local(): pl.pallas_call(functools.partial(kernel, (wins, bands, lats, members, lev...]
    ppermute x28 -> x0, waiting for transfers between devices: 100 us -> none  [the longest x6 74.9 us: passed_along(): return lax.ppermute(block, axis, route)]
    ppermute x28 -> x0, starting transfers between devices: 53 us -> none  [the longest x10 26.2 us: extended_2(): after = lax.ppermute(leading, axis, down)]
    psum x1 -> x0, blocking collectives: 42 us -> none  [local(): lax.psum((resid_local, search_local), ('win', 'lon', 'lat'))]
    dot_general x14 -> x0, matrix products: 27.6 us -> none  [the longest x7 19.9 us: weight_for(): jnp.einsum('j,jpq->pq', match, tiles, preferred_element_type=jnp.float32)]
    unnamed x46 -> x36, local copies, waits for them, and re-layouts: 4.26 us -> 16.5 us
    reduce_sum x5 -> x0, other arithmetic: 6.33 us -> none  [the longest x1 1.62 us: local(): jnp.sum(search_incr * search_incr)]
    convert_element_type x2 -> x0, other arithmetic: 2.6 us -> none  [the longest x1 2.46 us: localize(): products = (members * search[None]).astype(jnp.bfloat16)]
  transfers between devices with their start and end apart: 28 -> 0, of which waited for: 6 -> 0; matrix products, arithmetic and copies ran while one was open for 14% -> 0% of each run, Pallas kernels for 0% -> 0%
where the time goes in v1:
time: 126 us; the launch traced here: 125 us
  Pallas kernels  108 us (86%)
  local copies, waits for them, and re-layouts  16.5 us (13%)
    pallas_call x1, Pallas kernels, local(): pl.pallas_call(functools.partial(kernel, (wins, bands, lats, members, lev...  108 us
    unnamed x36, local copies, waits for them, and re-layouts  16.5 us

profile of v1, /device:TPU:0, one launch (start us, length us, event | category | flops | bytes accessed | tf_op | source)
XLA Modules:
  0.0 125.0 jit_solution(8925287026982338031)
XLA Ops:
  0.6 0.0 copy-start
  0.6 1.7 %copy-done = bf16[1,5,512,512]{3,2,1,0:T(8,128)(2,1)S(1)} copy-done((bf16[1,5,512,512]{3,2,1,0:T(8,128)(2,1)S(1)}, bf16[1,5,512,512]{3,2,1,0:T(8,128)(2,1)}, u32[]{:S(2)}) %copy-start) | copy-done | bytes 2621464
  2.4 0.0 copy-start.1
  2.4 1.2 copy-done.1
  3.6 0.9 copy-done.2
  4.5 0.0 copy-start.3
  4.5 0.8 copy-done.3
  5.3 0.0 copy-start.4
  5.3 0.8 copy-done.4
  6.0 0.0 copy-start.5
  6.0 0.8 copy-done.5
  6.8 0.0 copy-start.6
  6.8 0.8 copy-done.6
  7.6 0.8 copy-done.7
  8.3 0.0 copy-start.8
  8.3 0.8 copy-done.8
  9.1 0.0 copy-start.9
  9.1 0.8 copy-done.9
  9.8 0.0 copy-start.10
  9.8 0.8 copy-done.10
  10.6 0.0 copy-start.11
  10.6 0.8 copy-done.11
  11.3 0.8 copy-done.12
  12.1 0.8 copy-done.13
  12.9 0.7 copy-done.14
  13.5 107.8 %shard_map.190 = (f32[64,128]{1,0:T(8,128)S(1)}, f32[64,128]{1,0:T(8,128)S(1)}, f32[64,128]{1,0:T(8,128)S(1)}, f32[64,128]{1,0:T(8,128)S(1)}, f32[64,128]{1,0:T(8,128)S(1)}, /*index=5*/f32[64,128]{1,0:T(8,128)S(1)}) custom-call(f32[64,128]{1,0:T(8,128)S(1)} %bitcast.23, f32[64,128]{1,0:T(8,128)S(1)} %bitcast.24, f32[64,128]{1,0:T(8,128)S(1)} %bitcast.25, ...), custom_call_target="tpu_custom_call" | custom-call | tf_op jit(solution)/shard_map/pallas_call | solution.py:329
  121.3 0.6 copy.33
  121.9 0.6 copy.34
  122.6 0.6 copy.35
  123.2 0.6 copy.36
  123.8 0.6 copy.37
  124.4 0.6 copy.38
  (5 shorter events, 0.0 us)
Async XLA Ops:
  0.6 1.7 %copy-start = (bf16[1,5,512,512]{3,2,1,0:T(8,128)(2,1)S(1)}, bf16[1,5,512,512]{3,2,1,0:T(8,128)(2,1)}, u32[]{:S(2)}) copy-start(bf16[1,5,512,512]{3,2,1,0:T(8,128)(2,1)} %param.29) | copy-start | bytes 7864324
  2.4 1.2 copy-start.1
  3.6 0.9 copy-start.2
  4.5 0.8 copy-start.3
  5.3 0.8 copy-start.4
  6.0 0.8 copy-start.5
  6.8 0.8 copy-start.6
  7.6 0.8 copy-start.7
  8.3 0.8 copy-start.8
  9.1 0.8 copy-start.9
  9.8 0.8 copy-start.10
  10.6 0.8 copy-start.11
  11.3 0.8 copy-start.12
  12.1 0.8 copy-start.13
  12.9 0.7 copy-start.14

commit v2 on v1

v2 whole, which is shorter than its diff:
```python
import functools

import jax
import jax.numpy as jnp
from jax import lax
from jax.experimental import pallas as pl
from jax.experimental.pallas import tpu as pltpu
from jax.sharding import PartitionSpec as P

CHUNKS = 8
EARLY = 2
WEIGHTS = 4
LAG = 3
LANES = 128
MESH = pl.DeviceIdType.MESH
BF16 = jnp.bfloat16
F32 = jnp.float32


def remote(src, dst, send, recv, where):
    return pltpu.make_async_remote_copy(
        src_ref=src,
        dst_ref=dst,
        send_sem=send,
        recv_sem=recv,
        device_id=where,
        device_id_type=MESH,
    )


def kernel(
    sizes,
    dual_state_h, dual_obs_h, increment_h,
    resid_dual_h, resid_obs_h, resid_incr_h,
    search_dual_h, search_obs_h, search_incr_h,
    ens_h, coefs_h, obs_weight_h, obs_var_h, cols, vals_h,
    out,
    dual_state, dual_obs, increment,
    resid_dual, resid_obs, resid_incr,
    search_dual, search_obs, search_incr,
    ens, coefs, obs_weight, obs_var, vals, load,
    near, hold, near_s, own_s, w_home, w_out, w_in,
    g_own, g_lat, g_edge, g_side,
    part, part_lon, pair, part_col,
    moved, moved_in, acc, back, covar_flat,
    e_send, e_recv, s_send, s_recv, w_send, w_recv, f_send, f_recv, h_send, h_recv,
    g_send, g_recv, a_send, a_recv, b_send, b_recv,
    m_send, m_recv, r_send, r_recv,
):
    wins, bands, lats, members, levels, block = sizes
    colors = wins * lats
    pieces = block // LANES
    flat = levels * pieces
    rows = members * levels // CHUNKS
    group = rows // levels
    share = block // colors
    win = lax.axis_index("win")
    lon = lax.axis_index("lon")
    lat = lax.axis_index("lat")
    color = win * lats + lat

    loads = [
        pltpu.make_async_copy(source, target, load.at[k])
        for k, (source, target) in enumerate((
            (search_dual_h, search_dual), (search_incr_h, search_incr), (coefs_h, coefs),
            (vals_h, vals), (ens_h, ens), (search_obs_h, search_obs),
            (resid_dual_h, resid_dual), (resid_obs_h, resid_obs), (resid_incr_h, resid_incr),
            (dual_state_h, dual_state), (dual_obs_h, dual_obs), (increment_h, increment),
            (obs_weight_h, obs_weight), (obs_var_h, obs_var),
        ))
    ]
    for copy in loads:
        copy.start()

    def at(lon_step=0, other_lat=False, win_step=0):
        return {
            "win": lax.rem(win + win_step + wins, wins),
            "lon": lax.rem(lon + lon_step + bands, bands),
            "lat": 1 - lat if other_lat else lat,
        }

    def peer(step):
        index = lax.rem(color + step, colors)
        return index, {"win": index // lats, "lon": lon, "lat": lax.rem(index, lats)}

    barrier = pltpu.get_barrier_semaphore()
    greeted = [at(step) for step in range(1, bands)]
    greeted += [peer(step)[1] for step in range(1, colors)]
    greeted += [at(1, True), at(-1, True)]
    for where in greeted:
        pl.semaphore_signal(barrier, inc=1, device_id=where, device_id_type=MESH)

    def rows_of(ref, base):
        return [ref[pl.ds(base + j, levels, stride=pieces), :] for j in range(pieces)]

    for copy in loads[:3]:
        copy.wait()
    for j, (u, v) in enumerate(zip(rows_of(search_dual, 0), rows_of(search_incr, 0))):
        own_s[:, pl.ds(j * LANES, LANES)] = u
        g_own[0, :, pl.ds(j * LANES, LANES)] = v
        g_own[1, :, pl.ds(j * LANES, LANES)] = u
    for c in range(5):
        for j, value in enumerate(rows_of(coefs, c * flat)):
            g_own[2 + c, :, pl.ds(j * LANES, LANES)] = value
    lane = lax.broadcasted_iota(jnp.int32, (levels, LANES), 1)
    lead = g_own[0, :, pl.ds(0, LANES)]
    last = pltpu.roll(g_own[0, :, pl.ds(block - LANES, LANES)], 2, 1)
    for k in range(1, 7):
        chosen = lane // 2 == k
        lead = jnp.where(chosen, pltpu.roll(g_own[k, :, pl.ds(0, LANES)], 2 * k, 1), lead)
        last = jnp.where(chosen, pltpu.roll(g_own[k, :, pl.ds(block - LANES, LANES)], 2 * k + 2, 1), last)
    g_edge[0] = last
    g_edge[1] = lead

    def slot_of(step):
        target = lax.rem(lon + step + bands, bands)
        slot = jnp.int32(0)
        found = jnp.int32(0)
        for j in range(vals.shape[0]):
            hit = cols[0, j] == target
            slot = jnp.where(hit, j, slot)
            found = jnp.where(hit, 1, found)
        return slot, found > 0

    mine = pl.ds(pl.multiple_of(color * share, share), share)
    loads[3].wait()
    for k, step in enumerate((1, 3, -2, -3)):
        slot, found = slot_of(step)
        w_out[k] = jnp.where(found, vals[slot, mine, :], jnp.zeros((share, block), BF16))
    loads[4].wait()

    pl.semaphore_wait(barrier, len(greeted))

    started = []

    def go(copy):
        copy.start()
        started.append(copy)

    ways = (1, -2)
    for k, way in enumerate(ways):
        go(remote(own_s, near_s.at[k], s_send.at[k], s_recv.at[k], at(way)))
        both = pl.ds(2 * k, 2)
        go(remote(w_out.at[both], w_in.at[both, mine], w_send.at[k], w_recv.at[k], at(way)))
    go(remote(g_own, g_lat, g_send.at[0], g_recv.at[0], at(0, True)))

    def edge(side, other):
        n = 1 + 2 * side + other
        way = 1 - 2 * side
        return remote(g_edge.at[side], g_side.at[side, other], g_send.at[n], g_recv.at[n], at(way, other == 1))

    for side in range(2):
        for other in range(2):
            go(edge(side, other))

    parity = lax.rem(lon, 2)
    even = parity == 0

    def lines(t):
        return pl.ds(pl.multiple_of(t * rows, rows), rows)

    def halves(t):
        return pl.ds(pl.multiple_of(t // 2 * rows, rows), rows)

    def to_west(t):
        return remote(ens.at[lines(t)], near.at[1, lines(t)], e_send.at[0, t], e_recv.at[0, t], at(-2))

    def to_east(t):
        return remote(ens.at[lines(t)], near.at[0, lines(t)], e_send.at[1, t], e_recv.at[1, t], at(1))

    def to_relay(t):
        way = 3 * lax.rem(t, 2) - 1
        return remote(ens.at[lines(t)], hold.at[halves(t)], e_send.at[1, t], e_recv.at[2, t], at(way))

    def from_relay(t):
        return remote(hold.at[halves(t)], near.at[0, lines(t)], e_send.at[2, t], e_recv.at[1, t], at(2 - 3 * parity))

    def first_sends(t, carry):
        @pl.when(lat == 0)
        def _():
            to_west(t).start()

        @pl.when(even)
        def _():
            to_east(t).start()

        @pl.when(jnp.logical_not(even))
        def _():
            to_relay(t).start()

        @pl.when(lat != 0)
        def _():
            to_west(t).start()

        return carry

    lax.fori_loop(0, EARLY, first_sends, 0)

    for copy in loads[5:]:
        copy.wait()
    resid_sq = jnp.sum(resid_dual[...] ** 2 + resid_obs[...] ** 2 + resid_incr[...] ** 2)
    search_sq = jnp.sum(search_dual[...] ** 2 + search_obs[...] ** 2 + search_incr[...] ** 2)
    first_row = lax.broadcasted_iota(jnp.int32, (8, LANES), 0) == 0
    part[...] = jnp.where(first_row, resid_sq, search_sq)
    part_lon[lon] = part[...]
    for step in range(1, bands):
        go(remote(part, part_lon.at[lon], a_send.at[step], a_recv.at[lon], at(step)))

    for d, step in enumerate((0, -1, 2)):
        slot, found = slot_of(step)
        w_home[d] = jnp.where(found, vals[slot], jnp.zeros((block, block), BF16))
    acc[...] = jnp.zeros_like(acc)

    every = pl.ds(0, WEIGHTS)
    for k in range(2):
        both = pl.ds(2 * k, 2)
        remote(w_out.at[both], w_in.at[both, mine], w_send.at[k], w_recv.at[k], at(0)).wait_recv()
    spot = w_in.at[every, mine]
    for step in range(1, wins):
        go(remote(spot, spot, f_send.at[step], f_recv.at[win], at(0, False, step)))
    lax.fori_loop(EARLY, 2 * EARLY, first_sends, 0)

    remote(g_own, g_lat, g_send.at[0], g_recv.at[0], at(0)).wait_recv()
    for side in range(2):
        for other in range(2):
            edge(side, other).wait_recv()

    def wide(k, other):
        middle = g_lat if other else g_own
        before = pltpu.roll(g_side[0, other], LANES - 2 - 2 * k, 1)
        after = pltpu.roll(g_side[1, other], (LANES - 2 * k) % LANES, 1)
        return jnp.concatenate([before, middle[k], after], axis=1)

    span = block + 2 * LANES

    def east(x):
        return pltpu.roll(x, span - 1, 1)

    def west(x):
        return pltpu.roll(x, 1, 1)

    here = [wide(k, 0) for k in range(7)]
    over = [wide(k, 1) for k in range(7)]
    south_row = lat == 0
    cross = jnp.where(south_row, here[5], here[6])
    cross_over = jnp.where(south_row, over[6], over[5])

    def forward(v, beyond, c, between):
        return (0.5 + c[2]) * v + c[3] * east(v) + c[4] * west(v) + between * beyond

    def adjoint(u, beyond, c, between):
        return (0.5 + c[2]) * u + west(c[3] * u) + east(c[4] * u) + between * beyond

    once = forward(here[0], over[0], here, cross)
    once_over = forward(over[0], here[0], over, cross_over)
    twice = forward(once, once_over, here, cross)
    back_once = adjoint(here[1], over[1], here, cross_over)
    back_over = adjoint(over[1], here[1], over, cross)
    back_twice = adjoint(back_once, back_over, here, cross_over)
    for j in range(pieces):
        cut = slice((j + 1) * LANES, (j + 2) * LANES)
        moved[0, pl.ds(j, levels, stride=pieces), :] = twice[:, cut]
        moved[1, pl.ds(j, levels, stride=pieces), :] = back_twice[:, cut]
    for k, way in enumerate((1, -1)):
        go(remote(moved.at[k], moved_in.at[k], m_send.at[k], m_recv.at[k], at(0, False, way)))

    for step in range(1, bands):
        source = lax.rem(lon + step, bands)
        remote(part, part_lon.at[source], a_send.at[step], a_recv.at[source], at(0)).wait_recv()
    pair[...] = jnp.sum(part_lon[...], axis=0)
    part_col[color] = pair[...]
    for step in range(1, colors):
        _, where = peer(step)
        go(remote(pair, part_col.at[color], b_send.at[step], b_recv.at[color], where))

    for step in range(1, wins):
        source = lax.rem(win + step, wins)
        remote(spot, spot, f_send.at[step], f_recv.at[source], at(0)).wait_recv()

    def over_lat(w, holder):
        theirs = pl.ds(pl.multiple_of((w * lats + holder) * share, share), share)
        place = w_in.at[every, theirs]
        return remote(place, place, h_send.at[w], h_recv.at[w], at(0, True))

    for w in range(wins):
        go(over_lat(w, lat))
    lax.fori_loop(2 * EARLY, CHUNKS, first_sends, 0)
    for k in range(2):
        remote(own_s, near_s.at[k], s_send.at[k], s_recv.at[k], at(0)).wait_recv()

    def spread_of(t):
        def read(ref, search):
            member = ref[...].astype(F32).reshape(group, levels, block)
            product = (member * search[None]).astype(BF16).reshape(rows, block)
            return member, product

        def weigh(member, terms):
            total = sum(jnp.dot(p, w, preferred_element_type=F32) for p, w in terms)
            return jnp.sum(member * total.reshape(group, levels, block), axis=0)

        member, product = read(ens.at[lines(t)], own_s[...])
        first, first_product = read(near.at[0, lines(t)], near_s[0])
        second, second_product = read(near.at[1, lines(t)], near_s[1])
        acc[0] += weigh(member, ((product, w_home[0]), (first_product, w_home[1]), (second_product, w_home[2])))
        acc[1] += weigh(first, ((product, w_in[0]), (second_product, w_in[1])))
        acc[2] += weigh(second, ((product, w_in[2]), (first_product, w_in[3])))

    def step_of(t, carry):
        @pl.when(jnp.logical_and(t < CHUNKS, lax.rem(t, 2) == parity))
        def _():
            to_relay(t).wait_recv()
            from_relay(t).start()

        @pl.when(t == LAG)
        def _():
            for w in range(wins):
                over_lat(w, 1 - lat).wait_recv()

        @pl.when(t >= LAG)
        def _():
            to_west(t - LAG).wait_recv()
            to_east(t - LAG).wait_recv()
            spread_of(t - LAG)

        return carry

    lax.fori_loop(0, CHUNKS + LAG, step_of, 0)

    for k, way in enumerate(ways):
        go(remote(acc.at[1 + k], back.at[k], r_send.at[k], r_recv.at[k], at(-way)))

    for step in range(1, colors):
        source, where = peer(step)
        remote(pair, part_col.at[source], b_send.at[step], b_recv.at[source], where).wait_recv()
    sums = jnp.sum(part_col[...], axis=0)
    alpha = sums[0:1, :] / (sums[1:2, :] + 1e-6)

    out[0] = dual_state[...] + alpha * search_dual[...]
    out[1] = dual_obs[...] + alpha * search_obs[...]
    out[2] = increment[...] + alpha * search_incr[...]
    image_obs = obs_var[...] * search_obs[...] + obs_weight[...] * search_incr[...]
    out[4] = resid_obs[...] - alpha * image_obs
    for k in range(2):
        remote(moved.at[k], moved_in.at[k], m_send.at[k], m_recv.at[k], at(0)).wait_recv()
    later = jnp.where(win < wins - 1, moved_in[1], 0.0)
    image_incr = search_dual[...] - later + obs_weight[...] * search_obs[...]
    out[5] = resid_incr[...] - alpha * image_incr
    prior = jnp.where(win > 0, moved_in[0], 0.0)

    for k in range(2):
        remote(acc.at[1 + k], back.at[k], r_send.at[k], r_recv.at[k], at(0)).wait_recv()
    covar = (acc[0] + back[0] + back[1]) / (members - 1)
    for j in range(pieces):
        covar_flat[pl.ds(j, levels, stride=pieces), :] = covar[:, j * LANES:(j + 1) * LANES]
    image_dual = covar_flat[...] + search_incr[...] - prior
    out[3] = resid_dual[...] - alpha * image_dual

    for copy in started:
        copy.wait_send()

    def sent(t, carry):
        to_west(t).wait_send()
        to_east(t).wait_send()

        @pl.when(lax.rem(t, 2) == parity)
        def _():
            from_relay(t).wait_send()

        return carry

    lax.fori_loop(0, CHUNKS, sent, 0)


def local(wins, bands, lats, *args):
    fields = list(args)
    _, members, levels, _, block = args[9].shape
    flat = levels * block // LANES
    for k in (0, 1, 2, 3, 4, 5, 6, 7, 8, 11, 12):
        fields[k] = args[k].reshape(flat, LANES)
    fields[9] = args[9].reshape(members * levels, block)
    fields[10] = args[10].reshape(5 * flat, LANES)
    fields[14] = args[14][0]
    colors = wins * lats
    share = block // colors
    total = members * levels
    vmem = pl.BlockSpec(memory_space=pltpu.VMEM)
    specs = [pl.BlockSpec(memory_space=pl.ANY)] * 15
    specs[13] = pl.BlockSpec(memory_space=pltpu.SMEM)
    dma = pltpu.SemaphoreType.DMA
    pairs = [(3, CHUNKS), (2,), (2,), (wins,), (wins,), (5,), (bands,), (colors,), (2,), (2,)]
    out = pl.pallas_call(
        functools.partial(kernel, (wins, bands, lats, members, levels, block)),
        out_shape=jax.ShapeDtypeStruct((6, flat, LANES), F32),
        in_specs=specs,
        out_specs=vmem,
        scratch_shapes=[
            pltpu.VMEM(fields[k].shape, fields[k].dtype) for k in range(15) if k != 13
        ] + [
            dma((14,)),
            pltpu.VMEM((2, total, block), BF16),
            pltpu.VMEM((total // 2, block), BF16),
            pltpu.VMEM((2, levels, block), F32),
            pltpu.VMEM((levels, block), F32),
            pltpu.VMEM((3, block, block), BF16),
            pltpu.VMEM((WEIGHTS, share, block), BF16),
            pltpu.VMEM((WEIGHTS, block, block), BF16),
            pltpu.VMEM((7, levels, block), F32),
            pltpu.VMEM((7, levels, block), F32),
            pltpu.VMEM((2, levels, LANES), F32),
            pltpu.VMEM((2, 2, levels, LANES), F32),
            pltpu.VMEM((8, LANES), F32),
            pltpu.VMEM((bands, 8, LANES), F32),
            pltpu.VMEM((8, LANES), F32),
            pltpu.VMEM((colors, 8, LANES), F32),
            pltpu.VMEM((2, flat, LANES), F32),
            pltpu.VMEM((2, flat, LANES), F32),
            pltpu.VMEM((3, levels, block), F32),
            pltpu.VMEM((2, levels, block), F32),
            pltpu.VMEM((flat, LANES), F32),
        ] + [dma(shape) for shape in pairs for _ in range(2)],
        compiler_params=pltpu.CompilerParams(
            collective_id=0, has_side_effects=True, vmem_limit_bytes=60 * 1024 * 1024
        ),
    )(*fields)
    return tuple(out[k].reshape(args[0].shape) for k in range(6))


def solution(mesh):
    wins, bands, lats = (mesh.shape[name] for name in ("win", "lon", "lat"))
    field = P("win", None, "lat", "lon")
    deep = P("win", None, None, "lat", "lon")
    return jax.shard_map(
        functools.partial(local, wins, bands, lats),
        mesh=mesh,
        in_specs=(field,) * 9 + (deep, deep, field, field, P("lon", None), P("lon", None, None, None)),
        out_specs=(field,) * 6,
        check_vma=False,
    )
```

time: 126 us -> 68 us (0.54)
  Pallas kernels: 108 us -> 65.6 us
  local copies, waits for them, and re-layouts: 16.5 us -> 1.52 us
    pallas_call x1, Pallas kernels: 108 us -> 65.6 us  [local(): pl.pallas_call(functools.partial(kernel, (wins, bands, lats, members, lev...]
    unnamed x36 -> x0, local copies, waits for them, and re-layouts: 16.5 us -> none
    slice x0 -> x1, local copies, waits for them, and re-layouts: none -> 1.52 us  [local(): return tuple((out[k].reshape(args[0].shape) for k in range(6)))]
where the time goes in v2:
time: 68 us; the launch traced here: 67.8 us
  Pallas kernels  65.6 us (96%)
  local copies, waits for them, and re-layouts  1.52 us (2%)
    pallas_call x1, Pallas kernels, local(): pl.pallas_call(functools.partial(kernel, (wins, bands, lats, members, lev...  65.6 us
    slice x1, local copies, waits for them, and re-layouts, local(): return tuple((out[k].reshape(args[0].shape) for k in range(6)))  1.52 us

profile of v2, /device:TPU:0, one launch (start us, length us, event | category | flops | bytes accessed | tf_op | source)
XLA Modules:
  0.0 67.8 jit_solution(13889904027919768500)
XLA Ops:
  0.6 65.6 %shard_map.190 = f32[6,64,128]{2,1,0:T(8,128)} custom-call(f32[64,128]{1,0:T(8,128)} %bitcast.23, f32[64,128]{1,0:T(8,128)} %bitcast.24, f32[64,128]{1,0:T(8,128)} %bitcast.25, f32[64,128]{1,0:T(8,128)} %bitcast.26, f32[64,128]{1,0:T(8,128)} %bitcast.27, f32[64,128]{1,0:T(8,128)} %bitcast.28, f32[64,128]{1,0:T(8,128)} %bitcast.29, f32[64,128]{1,0:T(8,128)} %bitcast.30, ...), custom_call_target="tpu_custom_call" | custom-call | tf_op jit(solution)/shard_map/pallas_call | solution.py:391
  66.3 1.5 %fusion = (f32[1,64,128]{2,1,0:T(8,128)}, f32[1,64,128]{2,1,0:T(8,128)}, f32[1,64,128]{2,1,0:T(8,128)}, f32[1,64,128]{2,1,0:T(8,128)}, f32[1,64,128]{2,1,0:T(8,128)}, /*index=5*/f32[1,64,128]{2,1,0:T(8,128)}) fusion(f32[6,64,128]{2,1,0:T(8,128)} %shard_map.190), kind=kLoop, calls=%fused_computation | loop fusion | bytes 393216 | tf_op jit(solution)/shard_map/slice | solution.py:425
